TPU v7x, 256 devices: a whole 4x4x8 slice. The times are simulated.
256 devices in a mesh: row: 8 (over x, core), col: 8 (over y, z_lo), shard: 4 (over z_hi).
Axes of the slice: x: 4, y: 4, z: 8 (z_hi: 4, z_lo: 2; z = z_hi * 2 + z_lo), core: 2. Of those that a mesh axis runs over, the one named last changes fastest.
Arguments:
- tokens: bfloat16 [8, 8, 2048, 1024], P('row', 'col', 'shard'), may hold values from -6 to 6
- cotangent: bfloat16 [8, 8, 2048, 1024], P('row', 'col', 'shard'), may hold values from -6 to 6
- w_in: bfloat16 [8, 1024, 4096], P('row', 'shard'), may hold values from -0.1875 to 0.1875
- w_out: bfloat16 [8, 4096, 1024], P('col', None, 'shard'), may hold values from -0.09375 to 0.09375
- frag_index: int32 [16], replicated, may hold values from 0 to 3
- mom_in: float32 [8, 1024, 1024], P('row', 'shard'), may hold values from -4 to 4
- mom_out: float32 [8, 1024, 1024], P('col', None, 'shard'), may hold values from -4 to 4
Outputs:
- mixed: bfloat16 [8, 8, 2048, 1024], P('row', 'col', 'shard')
- new_in: bfloat16 [8, 1024, 1024], P('row', 'shard')
- new_mom_in: float32 [8, 1024, 1024], P('row', 'shard')
- new_out: bfloat16 [8, 1024, 1024], P('col', None, 'shard')
- new_mom_out: float32 [8, 1024, 1024], P('col', None, 'shard')
Inputs may be any that keep to these rules, and one draw needn't show every extreme that they name: `frag_index`: one fragment index per level-1 module, followed by one per level-2 module.
All inputs are finite; a program needn't handle non-finite values.
Results may differ from a plain program's by a relative error of at most 0.0061.
Values may be sent and summed in bfloat16 or wider, within the bound.
A program may use at most 192 MiB of HBM per device.

v0:
```python
import jax
import jax.numpy as jnp
from jax import lax
from jax.sharding import PartitionSpec as P

FU = 1024


EPS = 1e-06
INNER_LR = 0.05
MOMENTUM = 0.9
OUTER_LR = 0.7
GELU_SCALE = 0.7978845608028654
GELU_CUBIC = 0.044715


def gelu_parts(preact):
    tangent = jnp.tanh(GELU_SCALE * (preact + GELU_CUBIC * preact * preact * preact))
    value = 0.5 * preact * (1.0 + tangent)
    slope = 0.5 * (1.0 + tangent) + 0.5 * preact * (1.0 - tangent * tangent) * GELU_SCALE * (
        1.0 + 3.0 * GELU_CUBIC * preact * preact
    )
    return (value, slope)


def shards(tokens, cotangent, w_in, w_out, frag_index, mom_in, mom_out):
    stream = tokens[0, 0].astype(jnp.float32)
    cot_rows = cotangent[0, 0]
    normed = (stream * lax.rsqrt(jnp.mean(stream * stream, axis=-1, keepdims=True) + EPS)).astype(
        jnp.bfloat16
    )
    row_count = w_in.shape[1]
    start_in = frag_index[lax.axis_index("row")] * FU
    start_out = frag_index[lax.axis_size("row") + lax.axis_index("col")] * FU
    my_start = lax.axis_index("shard") * row_count
    preact = jnp.dot(
        normed,
        lax.all_gather(w_in, "shard", axis=1, tiled=True)[0],
        preferred_element_type=jnp.float32,
    )
    value, slope = gelu_parts(preact)
    hidden = value.astype(jnp.bfloat16)
    block = lax.all_gather(w_out, "shard", axis=2, tiled=True)[0]
    produced = jnp.dot(hidden, block, preferred_element_type=jnp.float32)
    out_sum = produced
    frag_rows = lax.dynamic_slice_in_dim(block, start_in, FU, 0)
    hid_grad = lax.dot_general(
        cot_rows, frag_rows, (((1,), (1,)), ((), ())), preferred_element_type=jnp.float32
    )
    out_sum, hid_grad = (out_sum, hid_grad)
    mixed = (stream + out_sum).astype(jnp.bfloat16)
    pre_grad = (hid_grad * lax.dynamic_slice_in_dim(slope, start_in, FU, 1)).astype(jnp.bfloat16)
    grad_in = lax.dot_general(
        normed, pre_grad, (((0,), (0,)), ((), ())), preferred_element_type=jnp.float32
    )
    hid_frag = lax.dynamic_slice_in_dim(hidden, start_out, FU, 1)
    grad_out = lax.dot_general(
        hid_frag, cot_rows, (((0,), (0,)), ((), ())), preferred_element_type=jnp.float32
    )
    whole_in = lax.psum(grad_in, ("col", "shard"))
    whole_out = lax.psum(grad_out, ("row", "shard"))
    summed_in = lax.dynamic_slice_in_dim(whole_in, my_start, row_count, 0)
    summed_out = lax.dynamic_slice_in_dim(whole_out, my_start, row_count, 1)
    delta_in = INNER_LR * summed_in
    delta_out = INNER_LR * summed_out
    new_mom_in = MOMENTUM * mom_in[0] + delta_in
    new_mom_out = MOMENTUM * mom_out[0] + delta_out
    in_frag = lax.dynamic_slice_in_dim(w_in[0], start_in, FU, 1).astype(jnp.float32)
    out_frag = lax.dynamic_slice_in_dim(w_out[0], start_out, FU, 0).astype(jnp.float32)
    new_in = (in_frag - OUTER_LR * (delta_in + MOMENTUM * new_mom_in)).astype(jnp.bfloat16)
    new_out = (out_frag - OUTER_LR * (delta_out + MOMENTUM * new_mom_out)).astype(jnp.bfloat16)
    return (mixed[None, None], new_in[None], new_mom_in[None], new_out[None], new_mom_out[None])


def solution(mesh):
    placed = (
        P("row", "col", "shard", None),
        P("row", "col", "shard", None),
        P("row", "shard", None),
        P("col", None, "shard"),
        P(),
        P("row", "shard", None),
        P("col", None, "shard"),
    )
    return jax.shard_map(
        shards,
        mesh=mesh,
        in_specs=placed,
        out_specs=(
            P("row", "col", "shard", None),
            P("row", "shard", None),
            P("row", "shard", None),
            P("col", None, "shard"),
            P("col", None, "shard"),
        ),
        check_vma=False,
    )
```

profile of v0, /device:TPU:1, one launch (start us, length us, event | category | flops | bytes accessed | tf_op | source)
XLA Modules:
  0.0 823.5 jit_solution(16795456990789895281)
XLA Ops:
  7.2 0.0 copy-start
  7.2 0.0 copy-start.4
  7.2 0.0 copy-start.1
  7.2 0.0 all-gather.3.cloned.1.call-start
  7.2 0.7 all-gather.3.cloned.1.call-update
  7.9 0.0 all-gather.5.cloned.1.call-start
  8.0 0.7 all-gather.5.cloned.1.call-update
  8.7 0.0 all-reduce.3.cloned.1.call-start
  8.7 0.0 copy-done.4
  8.7 0.6 fusion.60
  10.0 0.0 copy-done.1
  10.0 0.3 fusion.9
  10.3 158.6 %all-gather.3.cloned.1.call-done = bf16[1,1024,4096]{2,1,0:T(8,128)(2,1)} async-done(((bf16[1,256,4096]{2,1,0:T(8,128)(2,1)}), bf16[1,1024,4096]{2,1,0:T(8,128)(2,1)}) %all-gather.3.cloned.1.call-update) | async-done | bytes 8388624 | tf_op jit(solution)/shard_map/all_gather | solution.py:38
  168.9 20.0 %fusion.1 = (f32[512,4096]{1,0:T(8,128)}, f32[512,4096]{1,0:T(8,128)}, bf16[512,4096]{1,0:T(8,128)(2,1)}, f32[512,4096]{1,0:T(8,128)}, f32[512,4096]{1,0:T(8,128)}) fusion(bf16[1,1024,4096]{2,1,0:T(8,128)(2,1)} %all-gather.3.cloned.1.call-done, bf16[1,1,512,1024]{3,2,1,0:T(8,128)(2,1)S(1)} %copy-done.1, f32[512]{0:T(512)S(1)} %add_rsqrt_fusion), kind=kOutput, calls=%fused_computation.2 | convolution fusion | flops 4315414528 | bytes 47187968 | tf_op jit(solution)/shard_map/dot_general | solution.py:36
  188.9 139.7 %all-gather.5.cloned.1.call-done = bf16[1,4096,1024]{2,1,0:T(8,128)(2,1)} async-done(((bf16[1,4096,256]{2,1,0:T(8,128)(2,1)}), bf16[1,4096,1024]{2,1,0:T(8,128)(2,1)}) %all-gather.5.cloned.1.call-update) | async-done | bytes 8388624 | tf_op jit(solution)/shard_map/all_gather | solution.py:43
  328.6 0.0 copy-done
  328.6 8.8 %fusion.31 = f32[1024,1024]{1,0:T(8,128)} fusion(f32[512,4096]{1,0:T(8,128)} %get-tuple-element.6, s32[]{:T(128)S(6)} %select_n.20, f32[512,4096]{1,0:T(8,128)} %get-tuple-element.8, f32[512,4096]{1,0:T(8,128)} %get-tuple-element.15, f32[512,4096]{1,0:T(8,128)} %get-tuple-element.5, bf16[1,4096,1024]{2,1,0:T(8,128)(2,1)} %all-gather.5.cloned.1.call-done, ...), kind=kOutput, calls=%fused_computation.34 | convolution fusion | flops 2155347968 | bytes 16780288 | tf_op jit(solution)/shard_map/dot_general | solution.py:53
  337.4 0.0 all-reduce.3.cloned.1.call-update
  337.4 0.0 all-reduce.5.cloned.1.call-start
  338.1 4.5 fusion.42
  342.6 0.0 all-reduce.5.cloned.1.call-update
  342.6 0.0 copy-start.2
  342.7 10.2 %fusion.25 = bf16[1,1,512,1024]{3,2,1,0:T(8,128)(2,1)} fusion(bf16[512,4096]{1,0:T(8,128)(2,1)} %get-tuple-element.7, bf16[1,4096,1024]{2,1,0:T(8,128)(2,1)} %all-gather.5.cloned.1.call-done, bf16[1,1,512,1024]{3,2,1,0:T(8,128)(2,1)S(1)} %copy-done.1), kind=kOutput, calls=%fused_computation.33 | convolution fusion | flops 4296540160 | bytes 14680064 | tf_op jit(solution)/shard_map/dot_general | solution.py:44
  352.8 0.0 copy-start.3
  352.9 145.1 %all-reduce.3.cloned.1.call-done = f32[1024,1024]{1,0:T(8,128)} async-done(((f32[1024,1024]{1,0:T(8,128)}), f32[1024,1024]{1,0:T(8,128)}) %all-reduce.3.cloned.1.call-update) | async-done | bytes 4194320 | tf_op jit(solution)/shard_map/psum | solution.py:60
  497.9 0.0 copy-done.2
  498.0 2.8 fusion.49
  500.8 313.4 %all-reduce.5.cloned.1.call-done = f32[1024,1024]{1,0:T(8,128)} async-done(((f32[1024,1024]{1,0:T(8,128)}), f32[1024,1024]{1,0:T(8,128)}) %all-reduce.5.cloned.1.call-update) | async-done | bytes 4194320 | tf_op jit(solution)/shard_map/psum | solution.py:61
  814.2 0.0 copy-done.3
  814.2 2.8 fusion.50
  (1 shorter events, 0.0 us)
Async XLA Ops:
  7.2 321.5 %copy-start = (bf16[1,1,512,1024]{3,2,1,0:T(8,128)(2,1)S(1)}, bf16[1,1,512,1024]{3,2,1,0:T(8,128)(2,1)}, u32[]{:S(2)}) copy-start(bf16[1,1,512,1024]{3,2,1,0:T(8,128)(2,1)} %param.8) | copy-start | bytes 3145732
  7.2 1.6 copy-start.4
  7.2 2.8 copy-start.1
  7.2 161.7 %all-gather.3.cloned.1.call-start = ((), (), s32[]{:S(2)}) async-start(), calls=%async_computation | async-start | bytes 10485760 | tf_op jit(solution)/shard_map/all_gather | solution.py:38
  7.9 320.7 %all-gather.5.cloned.1.call-start = ((), (), s32[]{:S(2)}) async-start(), calls=%async_computation.1 | async-start | bytes 10485760 | tf_op jit(solution)/shard_map/all_gather | solution.py:43
  8.7 489.3 %all-reduce.3.cloned.1.call-start = ((), (), s32[]{:S(2)}) async-start(), calls=%async_computation.2 | async-start | bytes 8388608 | tf_op jit(solution)/shard_map/psum | solution.py:60
  337.4 476.7 %all-reduce.5.cloned.1.call-start = ((), (), s32[]{:S(2)}) async-start(), calls=%async_computation.3 | async-start | bytes 8388608 | tf_op jit(solution)/shard_map/psum | solution.py:61
  342.6 155.3 %copy-start.2 = (f32[1,256,1024]{2,1,0:T(8,128)S(1)}, f32[1,256,1024]{2,1,0:T(8,128)}, u32[]{:S(2)}) copy-start(f32[1,256,1024]{2,1,0:T(8,128)} %param.12) | copy-start | bytes 3145732
  352.8 461.3 %copy-start.3 = (f32[1,1024,256]{2,1,0:T(8,128)S(1)}, f32[1,1024,256]{2,1,0:T(8,128)}, u32[]{:S(2)}) copy-start(f32[1,1024,256]{2,1,0:T(8,128)} %param.13) | copy-start | bytes 3145732
Sparse Core Ops, SparseCore 0:
  9.8 159.0 all-gather.2
  170.7 157.8 all-gather.4
  337.6 160.3 all-reduce.2
  500.6 313.4 all-reduce.4
where the time goes:
time: 824 us
  waiting for transfers between devices  758 us (92%)
  matrix products  43.4 us (5%)
  between operations  15.1 us (2%)
    psum x1, waiting for transfers between devices, shards(): whole_out = lax.psum(grad_out, ('row', 'shard'))  313 us
    all_gather x1, waiting for transfers between devices, shards(): lax.all_gather(w_in, 'shard', axis=1, tiled=True)[0]  159 us
    psum x1, waiting for transfers between devices, shards(): whole_in = lax.psum(grad_in, ('col', 'shard'))  145 us
    all_gather x1, waiting for transfers between devices, shards(): block = lax.all_gather(w_out, 'shard', axis=2, tiled=True)[0]  140 us
    dot_general x1, matrix products, shards(): jnp.dot(normed, lax.all_gather(w_in, 'shard', axis=1, tiled=True)[0], pre...  20 us
  transfers between devices with their start and end apart: 4, of which 4 were waited for; matrix products, arithmetic and copies ran while one was open for 5% of the time, Pallas kernels for 0%

commit v1 on v0

v1 whole, which is shorter than its diff:
```python
import jax
import jax.numpy as jnp
from jax import lax
from jax.experimental import pallas as pl
from jax.experimental.pallas import tpu as pltpu
from jax.sharding import PartitionSpec as P

MESH = pl.DeviceIdType.MESH
BF, F32 = jnp.bfloat16, jnp.float32
FU = 1024
EPS = 1e-06
INNER_LR = 0.05
MOMENTUM = 0.9
OUTER_LR = 0.7
GELU_SCALE = 0.7978845608028654
GELU_CUBIC = 0.044715
DOUBLE = (False, False, True, True)


class Place:
    def __init__(p):
        p.r, p.c, p.s = lax.axis_index("row"), lax.axis_index("col"), lax.axis_index("shard")
        p.x, p.k, p.y, p.l = p.r // 2, p.r % 2, p.c // 2, p.c % 2
        p.turn = 2 * p.l - 1

    def near(p):
        return (p.r, p.y * 2 + 1 - p.l, (p.s + p.turn + 4) % 4)

    def twin(p):
        return (p.r, p.y * 2 + 1 - p.l, p.s)

    def at_y(p, d):
        return (p.r, ((p.y + d + 4) % 4) * 2 + p.l, p.s)

    def twin_y(p, d):
        return (p.r, ((p.y + d + 4) % 4) * 2 + 1 - p.l, p.s)

    def at_x(p, d):
        return (((p.x + d + 4) % 4) * 2 + p.k, p.c, p.s)

    def at_s(p, d):
        return (p.r, p.c, (p.s + d + 4) % 4)

    def twin_s(p, d):
        return (p.r, p.y * 2 + 1 - p.l, (p.s + d + 4) % 4)

    def sib(p):
        return (p.x * 2 + 1 - p.k, p.c, p.s)

    def partners(p):
        some = [p.twin(), p.sib()]
        some += [p.at_y(d) for d in (1, 2, 3)] + [p.at_x(d) for d in (1, 2, 3)] + [p.at_s(d) for d in (1, 2, 3)]
        some += [p.twin_s(d) for d in (1, 2, 3)]
        return some


class Copies:
    def __init__(self, send, recv):
        self.send, self.recv, self.sent, self.ids = send, recv, [], {}

    def at(self, name):
        return self.recv.at[self.ids.setdefault(name, len(self.ids))]

    def put(self, name, src, dst, dev):
        copy = pltpu.make_async_remote_copy(
            src_ref=src, dst_ref=dst, send_sem=self.send.at[len(self.sent)], recv_sem=self.at(name),
            device_id=dev, device_id_type=MESH,
        )
        copy.start()
        self.sent.append(copy)
        return copy

    def got(self, name, slot):
        pltpu.make_async_remote_copy(
            src_ref=slot, dst_ref=slot, send_sem=self.send.at[0], recv_sem=self.at(name),
            device_id=self.sent[0].device_id, device_id_type=MESH,
        ).wait_recv()

    def flush(self):
        for copy in self.sent:
            copy.wait_send()


def gelu(v):
    tangent = jnp.tanh(GELU_SCALE * (v + GELU_CUBIC * v * v * v))
    return tangent, 0.5 * v * (1.0 + tangent)


def slope_of(v, tangent):
    return 0.5 * (1.0 + tangent) + 0.5 * v * (1.0 - tangent * tangent) * GELU_SCALE * (
        1.0 + 3.0 * GELU_CUBIC * v * v
    )


def rows(start, size):
    return pl.ds(pl.multiple_of(start, size), size)


def kernel(
    frag, tok_hbm, cot_hbm, win_hbm, wout_hbm,
    mix_hbm, fin_hbm, fout_hbm,
    OWN, WIN, WOUT, TOK, COT, NORM, NT, HID, SLOPE, PG, GIF, GIB, RA, RB, RBR, FIN,
    GO, GOR, HT, GXF, GXB, RX, RSB, RSR, FOUT, MIX, WFRAG, HFRAG, HIDN,
    send, recv, local,
):
    p = Place()
    C = Copies(send, recv)
    y, s, r, x, k, l = p.y, p.s, p.r, p.x, p.k, p.l
    yp, ym, yf = (y + 1) % 4, (y + 3) % 4, (y + 2) % 4
    ci = frag[r]
    ej = frag[8 + p.c]
    te = lax.rem(ej - ci + 4, 4)
    quarter = [lax.rem(ci + t, 4) for t in range(4)]
    turned = [lax.rem(q - ci + 4, 4) for q in range(4)]

    fetch = []

    def load(src, dst):
        copy = pltpu.make_async_copy(src, dst, local.at[len(fetch)])
        copy.start()
        fetch.append(copy)
        return copy

    own_in = [load(win_hbm.at[0, :, pl.ds(q * 1024, 1024)], OWN.at[q]) for q in range(4)]
    tok_in = load(tok_hbm.at[0, 0], TOK)
    cot_in = load(cot_hbm.at[0, 0], COT)
    wout_in = [load(wout_hbm.at[0, pl.ds(q * 1024, 1024), :], WOUT.at[s, q]) for q in range(4)]

    barrier = pltpu.get_barrier_semaphore()
    partners = p.partners()
    for dev in partners:
        pl.semaphore_signal(barrier, inc=1, device_id=dev, device_id_type=MESH)
    pl.semaphore_wait(barrier, len(partners))

    near, twin, sib = p.near(), p.twin(), p.sib()
    shard = {"n": (s + p.turn + 4) % 4, "t": (s - p.turn + 4) % 4, "f": (s + 2) % 4}
    so = {"m": (s + 3) % 4, "p": (s + 1) % 4, "f": (s + 2) % 4}
    ox = {"0": r, "m": ((x + 3) % 4) * 2 + k, "p": ((x + 1) % 4) * 2 + k, "f": ((x + 2) % 4) * 2 + k}

    def wo(f, o, g=None):
        if g is None:
            return WOUT.at[f, o // 2, rows((o % 2) * 512, 512), :]
        return WOUT.at[f, o // 2, rows((o % 2) * 512 + g * 256, 256), :]

    mine = wout_hbm.at[0, rows(r * 512, 512), :]
    C.put("s1m", mine, wo(s, r), p.at_s(1))
    C.put("s1p", mine, wo(s, r), p.at_s(-1))

    def s_hop(side):
        if side == "m":
            C.got("s1m", wo(so["m"], r))
            C.put("s2m", wo(so["m"], r, 0), wo(so["m"], r, 0), p.at_s(1))
        else:
            C.got("s1p", wo(so["p"], r))
            C.put("s2p", wo(so["p"], r, 1), wo(so["p"], r, 1), p.at_s(-1))
        x_send(side)

    def s_last():
        C.got("s2m", wo(so["f"], r, 0))
        C.got("s2p", wo(so["f"], r, 1))
        x_send("f")

    def x_send(f):
        ref = wo(so[f], r)
        C.put(f"xm{f}", ref, ref, p.at_x(1))
        C.put(f"xp{f}", ref, ref, p.at_x(-1))
        C.put(f"c0{f}", ref, ref, sib)

    def x_hop(f):
        a, b = wo(so[f], ox["m"]), wo(so[f], ox["p"])
        C.got(f"xm{f}", a)
        ref = wo(so[f], ox["m"], 0)
        C.put(f"vm{f}", ref, ref, p.at_x(1))
        C.got(f"xp{f}", b)
        ref = wo(so[f], ox["p"], 1)
        C.put(f"vp{f}", ref, ref, p.at_x(-1))
        C.put(f"cm{f}", a, a, sib)
        C.put(f"cp{f}", b, b, sib)

    def x_last(f):
        C.got(f"vm{f}", wo(so[f], ox["f"], 0))
        C.got(f"vp{f}", wo(so[f], ox["f"], 1))
        ref = wo(so[f], ox["f"])
        C.put(f"cf{f}", ref, ref, sib)

    def core_last():
        for f in "mpf":
            for o, at in ox.items():
                C.got(f"c{o}{f}", wo(so[f], at + 1 - 2 * k))

    first, second = l, 1 - l

    def zc(t, f, h):
        if DOUBLE[t]:
            return WIN.at[t, y % 2 + 2 * h, rows(f * 256, 256), :]
        return WIN.at[t, y, rows(f * 256 + h * 128, 128), :]

    def z_start(t):
        ref = zc(t, s, first)
        C.put(f"z{t}nB", ref, ref, near)
        ref = zc(t, s, second)
        C.put(f"z{t}nA", ref, ref, near)

    def z_hop1(t):
        ref = zc(t, shard["n"], first)
        C.got(f"z{t}nA", ref)
        C.put(f"z{t}tB", ref, ref, twin)
        ref = zc(t, shard["n"], second)
        C.got(f"z{t}nB", ref)
        C.put(f"z{t}tA", ref, ref, twin)
        y_send(t, "n")

    def z_hop2(t):
        ref = zc(t, shard["t"], second)
        C.got(f"z{t}tB", ref)
        C.put(f"z{t}fA", ref, ref, near)
        C.got(f"z{t}tA", zc(t, shard["t"], first))
        y_send(t, "t")

    def z_hop3(t):
        ref = zc(t, shard["f"], first)
        C.got(f"z{t}fA", ref)
        C.put(f"z{t}fB", ref, ref, twin)

    def z_hop4(t):
        C.got(f"z{t}fB", zc(t, shard["f"], second))
        y_send(t, "f")

    def blk(t, u, f, h=None):
        if h is None:
            return WIN.at[t, u, rows(shard[f] * 256, 256), :]
        return WIN.at[t, u, rows(shard[f] * 256 + h * 128, 128), :]

    def from_m(t):
        return (y + 1) % 2 if DOUBLE[t] else ym

    def from_p(t):
        return (y + 1) % 2 + 2 if DOUBLE[t] else yp

    def y_send(t, f):
        a = blk(t, y % 2 if DOUBLE[t] else y, f)
        b = blk(t, y % 2 + 2 if DOUBLE[t] else y, f)
        C.put(f"y{t}{f}m", a, a, p.at_y(1))
        C.put(f"y{t}{f}p", b, b, p.at_y(-1))

    def y_hop(t, f):
        C.got(f"y{t}{f}m", blk(t, from_m(t), f))
        if not DOUBLE[t]:
            ref = blk(t, ym, f, 0)
            C.put(f"w{t}{f}m", ref, ref, p.at_y(1))
        C.got(f"y{t}{f}p", blk(t, from_p(t), f))
        if not DOUBLE[t]:
            ref = blk(t, yp, f, 1)
            C.put(f"w{t}{f}p", ref, ref, p.at_y(-1))

    def y_last(t):
        if not DOUBLE[t]:
            for f in "ntf":
                C.got(f"w{t}{f}m", blk(t, yf, f, 0))
                C.got(f"w{t}{f}p", blk(t, yf, f, 1))

    def place_own(t):
        block = OWN[quarter[t]]
        for u in range(4):
            WIN[t, u, rows(s * 256, 256), :] = block[:, u * 256 : u * 256 + 256]

    def normalize():
        @pl.loop(0, 8)
        def _(i):
            at = rows(i * 64, 64)
            stream = TOK[at, :].astype(F32)
            mean = jnp.mean(stream * stream, axis=-1, keepdims=True)
            NORM[at, :] = (stream * lax.rsqrt(mean + EPS)).astype(BF)

    def transpose_normed():
        for i in range(4):
            NT[:, i * 128 : i * 128 + 128] = NORM[i * 128 : i * 128 + 128, :].T

    def up(t, u):
        @pl.loop(0, 2)
        def _(i):
            at = rows(i * 256, 256)
            v = jnp.dot(NORM[at, :], WIN[t, u], preferred_element_type=F32)
            tangent, value = gelu(v)
            HID[t, at, rows(u * 256, 256)] = value.astype(BF)
            if t == 0:
                SLOPE[u, at, :] = slope_of(v, tangent)

    def up_all(t):
        for u in (y, ym, yp, yf):
            up(t, u)

    def take_fragment():
        for b in range(4):
            WFRAG[b] = WOUT[b, ci]

    def pre_grad(u):
        @pl.loop(0, 2)
        def _(i):
            at = rows(i * 256, 256)
            total = jnp.zeros((256, 256), F32)
            for b in range(4):
                total += lax.dot_general(
                    COT[at, b * 256 : b * 256 + 256],
                    WFRAG[b, rows(u * 256, 256), :],
                    (((1,), (1,)), ((), ())),
                    preferred_element_type=F32,
                )
            PG[u, at, :] = (total * SLOPE[u, at, :]).astype(BF)

    def grad_in(u, out):
        @pl.loop(0, 4)
        def _(i):
            at = rows(i * 256, 256)
            out[at, :] = jnp.dot(NT[at, :], PG[u], preferred_element_type=F32).astype(out.dtype)

    LO, HI = pl.ds(0, 512), pl.ds(512, 512)

    def in_start():
        pre_grad(yf)
        grad_in(yf, GIB.at[2])
        C.put("ai0", GIB.at[2, LO], RA.at[0], p.at_y(1))
        C.put("ai1", GIB.at[2, HI], RA.at[1], p.at_y(-1))
        pre_grad(yp)
        grad_in(yp, GIB.at[0])
        C.put("ai2", GIB.at[0, HI], RA.at[2], p.at_y(1))
        pre_grad(ym)
        grad_in(ym, GIB.at[1])
        C.put("ai3", GIB.at[1, LO], RA.at[3], p.at_y(-1))

    def in_relay():
        C.got("ai0", RA.at[0])
        GIB[0, LO, :] = (GIB[0, LO, :].astype(F32) + RA[0].astype(F32)).astype(BF)
        C.put("ai4", GIB.at[0, LO], RA.at[4], p.at_y(1))
        C.got("ai1", RA.at[1])
        GIB[1, HI, :] = (GIB[1, HI, :].astype(F32) + RA[1].astype(F32)).astype(BF)
        C.put("ai5", GIB.at[1, HI], RA.at[5], p.at_y(-1))
        pre_grad(y)
        grad_in(y, GIF)

    zs = [(d, e) for d in range(4) for e in range(2) if (d, e) != (0, 0)]

    def in_sum():
        C.got("ai2", RA.at[2])
        C.got("ai3", RA.at[3])
        C.got("ai4", RA.at[4])
        C.got("ai5", RA.at[5])
        RB[LO, :] = (GIF[LO, :] + RA[3].astype(F32) + RA[4].astype(F32)).astype(BF)
        RB[HI, :] = (GIF[HI, :] + RA[2].astype(F32) + RA[5].astype(F32)).astype(BF)
        for n, (d, e) in enumerate(zs):
            piece = rows(((s + d) % 4) * 256 + (l + e - 2 * l * e) * 128, 128)
            dev = p.at_s(d) if e == 0 else p.twin_s(d)
            C.put(f"bi{n}", RB.at[piece], RBR.at[n], dev)

    def in_result():
        total = RB[rows(s * 256 + l * 128, 128), :].astype(F32)
        for n in range(7):
            C.got(f"bi{n}", RBR.at[n])
            total += RBR[n].astype(F32)
        FIN[y, l] = total.astype(BF)
        ref = FIN.at[y, l]
        C.put("ct", ref, ref, twin)
        C.put("cm0", ref, ref, p.at_y(1))
        C.put("cp0", ref, ref, p.at_y(-1))

    def in_spread():
        other = FIN.at[y, 1 - l]
        C.got("ct", other)
        C.put("cm1", other, other, p.at_y(1))
        C.put("cp1", other, other, p.at_y(-1))
        C.got("cm0", FIN.at[ym, l])
        ref = FIN.at[ym, l]
        C.put("cf0", ref, ref, p.at_y(1))
        C.got("cp0", FIN.at[yp, l])
        C.got("cp1", FIN.at[yp, 1 - l])
        ref = FIN.at[yp, 1 - l]
        C.put("cf1", ref, ref, p.at_y(-1))
        C.got("cm1", FIN.at[ym, 1 - l])
        C.got("cf0", FIN.at[yf, l])
        C.got("cf1", FIN.at[yf, 1 - l])

    def grad_out(half, out):
        for v in range(2):
            u = half * 2 + v
            HT[...] = HFRAG[:, rows(u * 256, 256)].T

            @pl.loop(0, 4)
            def _(i):
                at = rows(i * 256, 256)
                out[v, :, at] = jnp.dot(HT[...], COT[:, at], preferred_element_type=F32)

    def in_place():
        for q in range(4):
            HIDN[q] = HID[turned[q]]

    def out_start():
        HFRAG[...] = HID[te]
        grad_out(1 - k, GO.at[1])
        C.put("g0", GO.at[1], GOR, sib)
        grad_out(k, GO.at[0])

    def part(d):
        o = (x + d) % 4
        return o // 2, rows((o % 2) * 128, 128)

    def out_reduce():
        C.got("g0", GOR)
        for slot, d in ((2, 2), (0, 1), (1, 3), (None, 0)):
            b, at = part(d)
            total = GO[0, b, at, :] + GOR[b, at, :]
            if slot is None:
                GXF[...] = total
            else:
                GXB[slot] = total.astype(BF)
            if slot == 2:
                C.put("gx0", GXB.at[2, pl.ds(0, 64)], RX.at[0], p.at_x(1))
                C.put("gx1", GXB.at[2, pl.ds(64, 64)], RX.at[1], p.at_x(-1))
            if slot == 0:
                C.put("gx2", GXB.at[0, pl.ds(64, 64)], RX.at[2], p.at_x(1))
            if slot == 1:
                C.put("gx3", GXB.at[1, pl.ds(0, 64)], RX.at[3], p.at_x(-1))

    def out_relay():
        C.got("gx0", RX.at[0])
        GXB[0, 0:64, :] = (GXB[0, 0:64, :].astype(F32) + RX[0].astype(F32)).astype(BF)
        C.put("gx4", GXB.at[0, pl.ds(0, 64)], RX.at[4], p.at_x(1))
        C.got("gx1", RX.at[1])
        GXB[1, 64:128, :] = (GXB[1, 64:128, :].astype(F32) + RX[1].astype(F32)).astype(BF)
        C.put("gx5", GXB.at[1, pl.ds(64, 64)], RX.at[5], p.at_x(-1))

    def out_sum():
        for n in (2, 3, 4, 5):
            C.got(f"gx{n}", RX.at[n])
        for b in range(4):
            at = pl.ds(b * 256, 256)
            RSB[b, 0:64, :] = (GXF[0:64, at] + RX[3, :, at].astype(F32) + RX[4, :, at].astype(F32)).astype(BF)
            RSB[b, 64:128, :] = (GXF[64:128, at] + RX[2, :, at].astype(F32) + RX[5, :, at].astype(F32)).astype(BF)
        for d in (2, 1, 3):
            C.put(f"gs{d}", RSB.at[(s + d) % 4], RSR.at[d - 1], p.at_s(d))

    def out_result():
        total = RSB[s].astype(F32)
        for d in (1, 2, 3):
            C.got(f"gs{d}", RSR.at[d - 1])
            total += RSR[d - 1].astype(F32)
        FOUT[k, x] = total.astype(BF)
        ref = FOUT.at[k, x]
        C.put("hm", ref, ref, p.at_x(1))
        C.put("hp", ref, ref, p.at_x(-1))
        C.put("hf", ref, ref, p.at_x(2))
        C.put("h0", ref, ref, sib)

    def out_spread():
        for n, d in (("m", 3), ("p", 1), ("f", 2)):
            ref = FOUT.at[k, (x + d) % 4]
            C.got("h" + n, ref)
            C.put("i" + n, ref, ref, sib)
        for n, d in (("h0", 0), ("im", 3), ("ip", 1), ("if", 2)):
            C.got(n, FOUT.at[1 - k, (x + d) % 4])

    def down(b):
        @pl.loop(0, 2)
        def _(i):
            at = rows(i * 256, 256)
            total = TOK[at, b * 256 : b * 256 + 256].astype(F32)
            for t in range(4):
                total += jnp.dot(
                    HIDN[t, at, :], WOUT[b, t], preferred_element_type=F32
                )
            MIX[at, b * 256 : b * 256 + 256] = total.astype(BF)

    for copy in own_in:
        copy.wait()
    place_own(0)
    z_start(0)
    for t in (1, 2, 3):
        place_own(t)
    tok_in.wait()
    normalize()
    z_hop1(0)
    s_hop("m")
    s_hop("p")
    z_hop2(0)
    z_start(1)
    transpose_normed()
    x_hop("m")
    z_hop3(0)
    z_hop4(0)
    z_hop1(1)
    s_last()
    y_hop(0, "n")
    y_hop(0, "t")
    x_hop("p")
    z_hop2(1)
    z_start(2)
    y_hop(0, "f")
    x_last("m")
    z_hop3(1)
    z_hop4(1)
    x_hop("f")
    x_last("p")
    z_hop1(2)
    y_last(0)
    y_hop(1, "n")
    y_hop(1, "t")
    up(0, y)
    up(0, ym)
    x_last("f")
    z_hop2(2)
    z_start(3)
    up(0, yp)
    up(0, yf)
    y_hop(1, "f")
    z_hop3(2)
    z_hop4(2)
    cot_in.wait()
    for copy in wout_in:
        copy.wait()
    core_last()
    take_fragment()
    in_start()
    z_hop1(3)
    y_last(1)
    up(1, y)
    up(1, ym)
    z_hop2(3)
    up(1, yp)
    up(1, yf)
    in_relay()
    for f in "ntf":
        y_hop(2, f)
    z_hop3(3)
    z_hop4(3)
    up_all(2)
    for f in "ntf":
        y_hop(3, f)
    up_all(3)
    out_start()
    in_sum()
    in_place()
    out_reduce()
    down(0)
    out_relay()
    down(1)
    out_sum()
    in_result()
    down(2)
    out_result()
    in_spread()
    down(3)
    out_spread()

    stores = []
    for n, (src, dst) in enumerate(((MIX, mix_hbm.at[0, 0]), (FIN, fin_hbm), (FOUT, fout_hbm))):
        copy = pltpu.make_async_copy(src, dst, local.at[len(fetch) + n])
        copy.start()
        stores.append(copy)
    C.flush()
    for copy in stores:
        copy.wait()


SCRATCH = [
    ((4, 256, 1024), BF),
    ((4, 4, 1024, 256), BF),
    ((4, 4, 1024, 256), BF),
    ((512, 1024), BF),
    ((512, 1024), BF),
    ((512, 1024), BF),
    ((1024, 512), BF),
    ((4, 512, 1024), BF),
    ((4, 512, 256), F32),
    ((4, 512, 256), BF),
    ((1024, 256), F32),
    ((3, 1024, 256), BF),
    ((6, 512, 256), BF),
    ((1024, 256), BF),
    ((7, 128, 256), BF),
    ((4, 2, 128, 256), BF),
    ((2, 2, 256, 1024), F32),
    ((2, 256, 1024), F32),
    ((256, 512), BF),
    ((128, 1024), F32),
    ((3, 128, 1024), BF),
    ((6, 64, 1024), BF),
    ((4, 128, 256), BF),
    ((3, 128, 256), BF),
    ((2, 4, 128, 256), BF),
    ((512, 1024), BF),
    ((4, 1024, 256), BF),
    ((512, 1024), BF),
    ((4, 512, 1024), BF),
]


def path_step(frag_index, tokens, cotangent, w_in, w_out):
    anywhere = pl.BlockSpec(memory_space=pl.ANY)
    return pl.pallas_call(
        kernel,
        out_shape=(
            jax.ShapeDtypeStruct((1, 1, 512, 1024), BF),
            jax.ShapeDtypeStruct((4, 2, 128, 256), BF),
            jax.ShapeDtypeStruct((2, 4, 128, 256), BF),
        ),
        in_specs=[pl.BlockSpec(memory_space=pltpu.SMEM)] + [anywhere] * 4,
        out_specs=(anywhere,) * 3,
        scratch_shapes=[pltpu.VMEM(shape, dtype) for shape, dtype in SCRATCH]
        + [pltpu.SemaphoreType.DMA((180,)), pltpu.SemaphoreType.DMA((180,)), pltpu.SemaphoreType.DMA((16,))],
        compiler_params=pltpu.CompilerParams(
            collective_id=0, has_side_effects=True, vmem_limit_bytes=60 * 2**20
        ),
        cost_estimate=pl.CostEstimate(flops=12 * 2**30, bytes_accessed=24 * 2**20, transcendentals=2**21),
        name="path_step",
    )(frag_index, tokens, cotangent, w_in, w_out)


def shards(tokens, cotangent, w_in, w_out, frag_index, mom_in, mom_out):
    start_in = frag_index[lax.axis_index("row")] * FU
    start_out = frag_index[lax.axis_size("row") + lax.axis_index("col")] * FU
    mixed, sums_in, sums_out = path_step(frag_index, tokens, cotangent, w_in, w_out)
    summed_in = sums_in.transpose(1, 2, 0, 3).reshape(256, FU).astype(F32)
    summed_out = sums_out.reshape(FU, 256).astype(F32)
    delta_in = INNER_LR * summed_in
    delta_out = INNER_LR * summed_out
    new_mom_in = MOMENTUM * mom_in[0] + delta_in
    new_mom_out = MOMENTUM * mom_out[0] + delta_out
    in_frag = lax.dynamic_slice_in_dim(w_in[0], start_in, FU, 1).astype(F32)
    out_frag = lax.dynamic_slice_in_dim(w_out[0], start_out, FU, 0).astype(F32)
    new_in = (in_frag - OUTER_LR * (delta_in + MOMENTUM * new_mom_in)).astype(BF)
    new_out = (out_frag - OUTER_LR * (delta_out + MOMENTUM * new_mom_out)).astype(BF)
    return (mixed, new_in[None], new_mom_in[None], new_out[None], new_mom_out[None])


def solution(mesh):
    placed = (
        P("row", "col", "shard", None),
        P("row", "col", "shard", None),
        P("row", "shard", None),
        P("col", None, "shard"),
        P(),
        P("row", "shard", None),
        P("col", None, "shard"),
    )
    return jax.shard_map(
        shards,
        mesh=mesh,
        in_specs=placed,
        out_specs=(
            P("row", "col", "shard", None),
            P("row", "shard", None),
            P("row", "shard", None),
            P("col", None, "shard"),
            P("col", None, "shard"),
        ),
        check_vma=False,
    )
```

time: 824 us -> 150 us (0.18)
  waiting for transfers between devices: 758 us -> 0 us
  Pallas kernels: 0 us -> 138 us
  matrix products: 43.4 us -> 0 us
  between operations: 15.1 us -> 2.03 us
    psum x2 -> x0, waiting for transfers between devices: 458 us -> none  [the longest x1 313 us: shards(): whole_out = lax.psum(grad_out, ('row', 'shard'))]
    all_gather x2 -> x0, waiting for transfers between devices: 298 us -> none  [the longest x1 159 us: shards(): lax.all_gather(w_in, 'shard', axis=1, tiled=True)[0]]
    pallas_call x0 -> x1, Pallas kernels: none -> 138 us  [path_step(): pl.pallas_call(kernel, out_shape=(jax.ShapeDtypeStruct((1, 1, 512, 1024),...]
    dot_general x4 -> x0, matrix products: 43.4 us -> none  [the longest x1 20 us: shards(): jnp.dot(normed, lax.all_gather(w_in, 'shard', axis=1, tiled=True)[0], pre...]
  transfers between devices with their start and end apart: 4 -> 0, of which waited for: 4 -> 0; matrix products, arithmetic and copies ran while one was open for 5% -> 0% of each run, Pallas kernels for 0% -> 0%
where the time goes in v1:
time: 150 us
  Pallas kernels  138 us (92%)
  other arithmetic  6.41 us (4%)
  local copies, waits for them, and re-layouts  3.53 us (2%)
  between operations  2.03 us (1%)
    pallas_call x1, Pallas kernels, path_step(): pl.pallas_call(kernel, out_shape=(jax.ShapeDtypeStruct((1, 1, 512, 1024),...  138 us

profile of v1, /device:TPU:1, one launch (start us, length us, event | category | flops | bytes accessed | tf_op | source)
XLA Modules:
  0.0 150.2 jit_solution(11912909800720820419)
XLA Ops:
  0.6 1.3 fusion
  3.3 138.3 %path_step.1 = (bf16[1,1,512,1024]{3,2,1,0:T(8,128)(2,1)}, bf16[4,2,128,256]{3,2,1,0:T(8,128)(2,1)}, bf16[2,4,128,256]{3,2,1,0:T(8,128)(2,1)}) custom-call(s32[16]{0:T(128)} %frag.1, bf16[1,1,512,1024]{3,2,1,0:T(8,128)(2,1)} %tok_hbm.1, bf16[1,1,512,1024]{3,2,1,0:T(8,128)(2,1)} %cot_hbm.1, bf16[1,256,4096]{2,1,0:T(8,128)(2,1)} %win_hbm.1, ...), custom_call_target="tpu_custom_call" | custom-call | flops 12884901888 | bytes 25165824 | tf_op jit(solution)/shard_map/path_step/pallas_call | solution.py:598
  141.5 1.1 multiply_bitcast_fusion
  142.7 0.0 copy-start
  142.7 0.7 copy.12
  143.4 0.5 mul.86
  143.9 0.0 copy-done
  143.9 0.0 copy-start.3
  143.9 0.0 copy-start.1
  144.0 2.6 %subtract_convert_fusion.1 = (bf16[1,256,1024]{2,1,0:T(8,128)(2,1)}, f32[1,256,1024]{2,1,0:T(8,128)}) fusion(f32[1,256,1024]{2,1,0:T(8,128)S(1)} %mul.86, bf16[1,256,4096]{2,1,0:T(8,128)(2,1)} %win_hbm.1, s32[]{:T(128)S(6)} %select_n.13, f32[1,256,1024]{2,1,0:T(8,128)S(1)} %copy-done), kind=kLoop, calls=%fused_computation.3 | loop fusion | flops 2097152 | bytes 4194308 | tf_op jit(solution)/shard_map/convert_element_type | solution.py:629
  146.6 0.0 copy-done.3
  146.6 0.1 convert_multiply_fusion
  146.7 0.0 copy-done.1
  146.7 0.0 copy-start.2
  146.7 2.6 %subtract_convert_fusion = (bf16[1,1024,256]{2,1,0:T(8,128)(2,1)}, f32[1,1024,256]{2,1,0:T(8,128)}) fusion(f32[1,1024,256]{2,1,0:T(8,128)S(1)} %bitcast.5, bf16[1,4096,256]{2,1,0:T(8,128)(2,1)} %wout_hbm.1, s32[]{:T(128)S(6)} %select_n.15, f32[1,1024,256]{2,1,0:T(8,128)S(1)} %copy-done.1), kind=kLoop, calls=%fused_computation | loop fusion | flops 2097152 | bytes 4194308 | tf_op jit(solution)/shard_map/convert_element_type | solution.py:630
  149.3 0.0 copy-done.2
  149.3 1.0 copy.14
Async XLA Ops:
  142.7 1.2 copy-start
  143.9 2.6 %copy-start.3 = (bf16[2,4,128,256]{3,2,1,0:T(8,128)(2,1)S(1)}, bf16[2,4,128,256]{3,2,1,0:T(8,128)(2,1)}, u32[]{:S(2)}) copy-start(bf16[2,4,128,256]{3,2,1,0:T(8,128)(2,1)} %get-tuple-element.10) | copy-start | bytes 1572868
  143.9 2.7 %copy-start.1 = (f32[1,1024,256]{2,1,0:T(8,128)S(1)}, f32[1,1024,256]{2,1,0:T(8,128)}, u32[]{:S(2)}) copy-start(f32[1,1024,256]{2,1,0:T(8,128)} %param.13) | copy-start | bytes 3145732
  146.7 2.6 %copy-start.2 = (bf16[1,1,512,1024]{3,2,1,0:T(8,128)(2,1)S(1)}, bf16[1,1,512,1024]{3,2,1,0:T(8,128)(2,1)}, u32[]{:S(2)}) copy-start(bf16[1,1,512,1024]{3,2,1,0:T(8,128)(2,1)} %get-tuple-element.22) | copy-start | bytes 3145732

commit v2 on v1

--- a/solution.py
+++ b/solution.py
@@ -113,7 +113,7 @@
     quarter = [lax.rem(ci + t, 4) for t in range(4)]
     turned = [lax.rem(q - ci + 4, 4) for q in range(4)]
 
-    fetch = []
+    fetch, mix_out = [], []
 
     def load(src, dst):
         copy = pltpu.make_async_copy(src, dst, local.at[len(fetch)])
@@ -142,23 +142,24 @@
             return WOUT.at[f, o // 2, rows((o % 2) * 512, 512), :]
         return WOUT.at[f, o // 2, rows((o % 2) * 512 + g * 256, 256), :]
 
-    mine = wout_hbm.at[0, rows(r * 512, 512), :]
-    C.put("s1m", mine, wo(s, r), p.at_s(1))
-    C.put("s1p", mine, wo(s, r), p.at_s(-1))
+    def s_start():
+        mine = wout_hbm.at[0, rows(r * 512, 512), :]
+        C.put("s1m", mine, wo(s, r), p.at_s(1))
+        C.put("s1p", mine, wo(s, r), p.at_s(-1))
 
     def s_hop(side):
         if side == "m":
             C.got("s1m", wo(so["m"], r))
-            C.put("s2m", wo(so["m"], r, 0), wo(so["m"], r, 0), p.at_s(1))
+            ref = wo(so["m"], r, 0)
+            C.put("s2m", ref, ref, p.at_s(1))
         else:
             C.got("s1p", wo(so["p"], r))
-            C.put("s2p", wo(so["p"], r, 1), wo(so["p"], r, 1), p.at_s(-1))
-        x_send(side)
+            ref = wo(so["p"], r, 1)
+            C.put("s2p", ref, ref, p.at_s(-1))
 
     def s_last():
         C.got("s2m", wo(so["f"], r, 0))
         C.got("s2p", wo(so["f"], r, 1))
-        x_send("f")
 
     def x_send(f):
         ref = wo(so[f], r)
@@ -184,6 +185,8 @@
         C.put(f"cf{f}", ref, ref, sib)
 
     def core_last():
+        for copy in wout_in:
+            copy.wait()
         for f in "mpf":
             for o, at in ox.items():
                 C.got(f"c{o}{f}", wo(so[f], at + 1 - 2 * k))
@@ -265,6 +268,8 @@
             WIN[t, u, rows(s * 256, 256), :] = block[:, u * 256 : u * 256 + 256]
 
     def normalize():
+        tok_in.wait()
+
         @pl.loop(0, 8)
         def _(i):
             at = rows(i * 64, 64)
@@ -286,9 +291,10 @@
             if t == 0:
                 SLOPE[u, at, :] = slope_of(v, tangent)
 
-    def up_all(t):
-        for u in (y, ym, yp, yf):
-            up(t, u)
+    def block_at(t, n):
+        if DOUBLE[t]:
+            return (y % 2, y % 2 + 2, (y + 1) % 2, (y + 1) % 2 + 2)[n]
+        return (y, ym, yp, yf)[n]
 
     def take_fragment():
         for b in range(4):
@@ -316,27 +322,27 @@
 
     LO, HI = pl.ds(0, 512), pl.ds(512, 512)
 
-    def in_start():
-        pre_grad(yf)
-        grad_in(yf, GIB.at[2])
-        C.put("ai0", GIB.at[2, LO], RA.at[0], p.at_y(1))
-        C.put("ai1", GIB.at[2, HI], RA.at[1], p.at_y(-1))
-        pre_grad(yp)
-        grad_in(yp, GIB.at[0])
-        C.put("ai2", GIB.at[0, HI], RA.at[2], p.at_y(1))
-        pre_grad(ym)
-        grad_in(ym, GIB.at[1])
-        C.put("ai3", GIB.at[1, LO], RA.at[3], p.at_y(-1))
-
-    def in_relay():
-        C.got("ai0", RA.at[0])
-        GIB[0, LO, :] = (GIB[0, LO, :].astype(F32) + RA[0].astype(F32)).astype(BF)
-        C.put("ai4", GIB.at[0, LO], RA.at[4], p.at_y(1))
-        C.got("ai1", RA.at[1])
-        GIB[1, HI, :] = (GIB[1, HI, :].astype(F32) + RA[1].astype(F32)).astype(BF)
-        C.put("ai5", GIB.at[1, HI], RA.at[5], p.at_y(-1))
-        pre_grad(y)
-        grad_in(y, GIF)
+    def in_part(n):
+        u = (yf, yp, ym, y)[n]
+        pre_grad(u)
+        grad_in(u, (GIB.at[2], GIB.at[0], GIB.at[1], GIF)[n])
+        if n == 0:
+            C.put("ai0", GIB.at[2, LO], RA.at[0], p.at_y(1))
+            C.put("ai1", GIB.at[2, HI], RA.at[1], p.at_y(-1))
+        if n == 1:
+            C.put("ai2", GIB.at[0, HI], RA.at[2], p.at_y(1))
+        if n == 2:
+            C.put("ai3", GIB.at[1, LO], RA.at[3], p.at_y(-1))
+
+    def in_relay(side):
+        if side == 0:
+            C.got("ai0", RA.at[0])
+            GIB[0, LO, :] = (GIB[0, LO, :].astype(F32) + RA[0].astype(F32)).astype(BF)
+            C.put("ai4", GIB.at[0, LO], RA.at[4], p.at_y(1))
+        else:
+            C.got("ai1", RA.at[1])
+            GIB[1, HI, :] = (GIB[1, HI, :].astype(F32) + RA[1].astype(F32)).astype(BF)
+            C.put("ai5", GIB.at[1, HI], RA.at[5], p.at_y(-1))
 
     zs = [(d, e) for d in range(4) for e in range(2) if (d, e) != (0, 0)]
 
@@ -368,43 +374,50 @@
         C.got("ct", other)
         C.put("cm1", other, other, p.at_y(1))
         C.put("cp1", other, other, p.at_y(-1))
+
+    def in_spread_more():
         C.got("cm0", FIN.at[ym, l])
         ref = FIN.at[ym, l]
         C.put("cf0", ref, ref, p.at_y(1))
-        C.got("cp0", FIN.at[yp, l])
         C.got("cp1", FIN.at[yp, 1 - l])
         ref = FIN.at[yp, 1 - l]
         C.put("cf1", ref, ref, p.at_y(-1))
+        C.got("cp0", FIN.at[yp, l])
         C.got("cm1", FIN.at[ym, 1 - l])
+
+    def in_last():
         C.got("cf0", FIN.at[yf, l])
         C.got("cf1", FIN.at[yf, 1 - l])
 
-    def grad_out(half, out):
-        for v in range(2):
-            u = half * 2 + v
-            HT[...] = HFRAG[:, rows(u * 256, 256)].T
-
-            @pl.loop(0, 4)
-            def _(i):
-                at = rows(i * 256, 256)
-                out[v, :, at] = jnp.dot(HT[...], COT[:, at], preferred_element_type=F32)
+    def grad_out(half, v, out):
+        HT[...] = HFRAG[:, rows((half * 2 + v) * 256, 256)].T
+
+        @pl.loop(0, 4)
+        def _(i):
+            at = rows(i * 256, 256)
+            out[v, :, at] = jnp.dot(HT[...], COT[:, at], preferred_element_type=F32)
 
     def in_place():
         for q in range(4):
             HIDN[q] = HID[turned[q]]
 
-    def out_start():
-        HFRAG[...] = HID[te]
-        grad_out(1 - k, GO.at[1])
-        C.put("g0", GO.at[1], GOR, sib)
-        grad_out(k, GO.at[0])
+    def out_start(v):
+        if v == 0:
+            HFRAG[...] = HID[te]
+        grad_out(1 - k, v, GO.at[1])
+        C.put(f"g{v}", GO.at[1, v], GOR.at[v], sib)
+
+    def out_own():
+        for v in range(2):
+            grad_out(k, v, GO.at[0])
 
     def part(d):
         o = (x + d) % 4
         return o // 2, rows((o % 2) * 128, 128)
 
     def out_reduce():
-        C.got("g0", GOR)
+        C.got("g0", GOR.at[0])
+        C.got("g1", GOR.at[1])
         for slot, d in ((2, 2), (0, 1), (1, 3), (None, 0)):
             b, at = part(d)
             total = GO[0, b, at, :] + GOR[b, at, :]
@@ -455,6 +468,8 @@
             ref = FOUT.at[k, (x + d) % 4]
             C.got("h" + n, ref)
             C.put("i" + n, ref, ref, sib)
+
+    def out_last():
         for n, d in (("h0", 0), ("im", 3), ("ip", 1), ("if", 2)):
             C.got(n, FOUT.at[1 - k, (x + d) % 4])
 
@@ -469,94 +484,115 @@
                 )
             MIX[at, b * 256 : b * 256 + 256] = total.astype(BF)
 
+        mix_out.append(load(MIX.at[:, pl.ds(b * 256, 256)], mix_hbm.at[0, 0, :, pl.ds(b * 256, 256)]))
+
+    s_start()
     for copy in own_in:
         copy.wait()
     place_own(0)
     z_start(0)
-    for t in (1, 2, 3):
-        place_own(t)
-    tok_in.wait()
+    place_own(1)
+    z_hop1(0)
+    z_start(1)
+    z_hop2(0)
+    place_own(2)
+    z_start(2)
+    z_hop1(1)
     normalize()
-    z_hop1(0)
+    z_hop3(0)
     s_hop("m")
+    x_send("m")
+    z_hop2(1)
+    y_hop(0, "t")
+    y_hop(0, "n")
     s_hop("p")
-    z_hop2(0)
-    z_start(1)
+    z_hop4(0)
+    x_send("p")
+    place_own(3)
     transpose_normed()
+    y_hop(1, "t")
+    y_hop(1, "n")
+    z_start(3)
+    z_hop1(2)
+    s_last()
+    x_send("f")
+    z_hop3(1)
+    y_hop(0, "f")
+    z_hop1(3)
     x_hop("m")
-    z_hop3(0)
-    z_hop4(0)
-    z_hop1(1)
-    s_last()
-    y_hop(0, "n")
-    y_hop(0, "t")
-    x_hop("p")
-    z_hop2(1)
-    z_start(2)
-    y_hop(0, "f")
-    x_last("m")
-    z_hop3(1)
+    z_hop2(2)
     z_hop4(1)
     x_hop("f")
+    z_hop3(2)
+    x_hop("p")
+    z_hop2(3)
+    y_hop(2, "n")
+    up(1, block_at(1, 0))
+    up(0, block_at(0, 1))
+    x_last("f")
+    x_last("m")
+    z_hop4(2)
+    up(0, block_at(0, 0))
     x_last("p")
-    z_hop1(2)
+    y_hop(2, "t")
+    z_hop3(3)
+    up(2, block_at(2, 0))
     y_last(0)
-    y_hop(1, "n")
-    y_hop(1, "t")
-    up(0, y)
-    up(0, ym)
-    x_last("f")
-    z_hop2(2)
-    z_start(3)
-    up(0, yp)
-    up(0, yf)
+    up(0, block_at(0, 3))
+    up(0, block_at(0, 2))
+    core_last()
     y_hop(1, "f")
-    z_hop3(2)
-    z_hop4(2)
+    take_fragment()
+    y_hop(2, "f")
+    y_hop(3, "t")
+    y_last(2)
+    z_hop4(3)
+    y_hop(3, "n")
+    up(3, block_at(3, 1))
     cot_in.wait()
-    for copy in wout_in:
-        copy.wait()
-    core_last()
-    take_fragment()
-    in_start()
-    z_hop1(3)
+    in_part(0)
     y_last(1)
-    up(1, y)
-    up(1, ym)
-    z_hop2(3)
-    up(1, yp)
-    up(1, yf)
-    in_relay()
-    for f in "ntf":
-        y_hop(2, f)
-    z_hop3(3)
-    z_hop4(3)
-    up_all(2)
-    for f in "ntf":
-        y_hop(3, f)
-    up_all(3)
-    out_start()
+    up(2, block_at(2, 3))
+    up(2, block_at(2, 1))
+    up(1, block_at(1, 2))
+    up(3, block_at(3, 0))
+    in_part(1)
+    in_part(2)
+    up(1, block_at(1, 1))
+    up(1, block_at(1, 3))
+    y_hop(3, "f")
+    y_last(3)
+    up(3, block_at(3, 2))
+    up(2, block_at(2, 2))
+    up(3, block_at(3, 3))
+    in_relay(1)
+    out_start(0)
+    in_relay(0)
+    out_start(1)
+    out_own()
+    in_part(3)
+    out_reduce()
     in_sum()
     in_place()
-    out_reduce()
+    down(1)
+    out_relay()
+    out_sum()
     down(0)
-    out_relay()
-    down(1)
-    out_sum()
+    down(3)
     in_result()
     down(2)
     out_result()
     in_spread()
-    down(3)
+    in_spread_more()
     out_spread()
-
-    stores = []
-    for n, (src, dst) in enumerate(((MIX, mix_hbm.at[0, 0]), (FIN, fin_hbm), (FOUT, fout_hbm))):
-        copy = pltpu.make_async_copy(src, dst, local.at[len(fetch) + n])
-        copy.start()
-        stores.append(copy)
+    out_last()
+    in_last()
+
+    stores = [load(FIN, fin_hbm), load(FOUT, fout_hbm)]
     C.flush()
     for copy in stores:
+        copy.wait()
+    for copy in mix_out:
         copy.wait()
 
 
@@ -605,7 +641,7 @@
         in_specs=[pl.BlockSpec(memory_space=pltpu.SMEM)] + [anywhere] * 4,
         out_specs=(anywhere,) * 3,
         scratch_shapes=[pltpu.VMEM(shape, dtype) for shape, dtype in SCRATCH]
-        + [pltpu.SemaphoreType.DMA((180,)), pltpu.SemaphoreType.DMA((180,)), pltpu.SemaphoreType.DMA((16,))],
+        + [pltpu.SemaphoreType.DMA((180,)), pltpu.SemaphoreType.DMA((180,)), pltpu.SemaphoreType.DMA((20,))],
         compiler_params=pltpu.CompilerParams(
             collective_id=0, has_side_effects=True, vmem_limit_bytes=60 * 2**20
         ),
@@ -614,21 +650,71 @@
     )(frag_index, tokens, cotangent, w_in, w_out)
 
 
+def outer_kernel(
+    frag, mix_hbm, sin_hbm, sout_hbm, win_hbm, wout_hbm, min_hbm, mout_hbm,
+    mixed, new_in, new_mom_in, new_out, new_mom_out,
+    SIN, SOUT, WI, WO, MI, MO, NI, NMI, NO, NMO, sems,
+):
+    start_in = pl.multiple_of(frag[lax.axis_index("row")] * FU, FU)
+    start_out = pl.multiple_of(frag[lax.axis_size("row") + lax.axis_index("col")] * FU, FU)
+    begun = []
+
+    def move(src, dst):
+        copy = pltpu.make_async_copy(src, dst, sems.at[len(begun)])
+        copy.start()
+        begun.append(copy)
+        return copy
+
+    first = [move(min_hbm.at[0], MI), move(win_hbm.at[0, :, pl.ds(start_in, FU)], WI), move(sin_hbm, SIN)]
+    second = [move(mout_hbm.at[0], MO), move(wout_hbm.at[0, pl.ds(start_out, FU), :], WO), move(sout_hbm, SOUT)]
+    last = [move(mix_hbm, mixed)]
+
+    def update(delta, mom, frag_now):
+        delta = INNER_LR * delta.astype(F32)
+        mom = MOMENTUM * mom + delta
+        return mom, (frag_now.astype(F32) - OUTER_LR * (delta + MOMENTUM * mom)).astype(BF)
+
+    for copy in first:
+        copy.wait()
+    for u in range(4):
+        for h in range(2):
+            at = (slice(h * 128, h * 128 + 128), slice(u * 256, u * 256 + 256))
+            NMI[at], NI[at] = update(SIN[u, h], MI[at], WI[at])
+    last += [move(NMI, new_mom_in.at[0]), move(NI, new_in.at[0])]
+    for copy in second:
+        copy.wait()
+    for h in range(2):
+        for o in range(4):
+            at = slice(h * 512 + o * 128, h * 512 + o * 128 + 128)
+            NMO[at, :], NO[at, :] = update(SOUT[h, o], MO[at, :], WO[at, :])
+    last += [move(NMO, new_mom_out.at[0]), move(NO, new_out.at[0])]
+    for copy in last:
+        copy.wait()
+
+
 def shards(tokens, cotangent, w_in, w_out, frag_index, mom_in, mom_out):
-    start_in = frag_index[lax.axis_index("row")] * FU
-    start_out = frag_index[lax.axis_size("row") + lax.axis_index("col")] * FU
     mixed, sums_in, sums_out = path_step(frag_index, tokens, cotangent, w_in, w_out)
-    summed_in = sums_in.transpose(1, 2, 0, 3).reshape(256, FU).astype(F32)
-    summed_out = sums_out.reshape(FU, 256).astype(F32)
-    delta_in = INNER_LR * summed_in
-    delta_out = INNER_LR * summed_out
-    new_mom_in = MOMENTUM * mom_in[0] + delta_in
-    new_mom_out = MOMENTUM * mom_out[0] + delta_out
-    in_frag = lax.dynamic_slice_in_dim(w_in[0], start_in, FU, 1).astype(F32)
-    out_frag = lax.dynamic_slice_in_dim(w_out[0], start_out, FU, 0).astype(F32)
-    new_in = (in_frag - OUTER_LR * (delta_in + MOMENTUM * new_mom_in)).astype(BF)
-    new_out = (out_frag - OUTER_LR * (delta_out + MOMENTUM * new_mom_out)).astype(BF)
-    return (mixed, new_in[None], new_mom_in[None], new_out[None], new_mom_out[None])
+    anywhere = pl.BlockSpec(memory_space=pl.ANY)
+    sizes = [
+        ((4, 2, 128, 256), BF), ((2, 4, 128, 256), BF), ((256, FU), BF), ((FU, 256), BF), ((256, FU), F32),
+        ((FU, 256), F32), ((256, FU), BF), ((256, FU), F32), ((FU, 256), BF), ((FU, 256), F32),
+    ]
+    return pl.pallas_call(
+        outer_kernel,
+        out_shape=(
+            jax.ShapeDtypeStruct((1, 1, 512, 1024), BF),
+            jax.ShapeDtypeStruct((1, 256, FU), BF),
+            jax.ShapeDtypeStruct((1, 256, FU), F32),
+            jax.ShapeDtypeStruct((1, FU, 256), BF),
+            jax.ShapeDtypeStruct((1, FU, 256), F32),
+        ),
+        in_specs=[pl.BlockSpec(memory_space=pltpu.SMEM)] + [anywhere] * 7,
+        out_specs=(anywhere,) * 5,
+        scratch_shapes=[pltpu.VMEM(shape, dtype) for shape, dtype in sizes] + [pltpu.SemaphoreType.DMA((12,))],
+        compiler_params=pltpu.CompilerParams(vmem_limit_bytes=60 * 2**20),
+        cost_estimate=pl.CostEstimate(flops=2**22, bytes_accessed=9 * 2**20, transcendentals=0),
+        name="outer_update",
+    )(frag_index, mixed, sums_in, sums_out, w_in, w_out, mom_in, mom_out)
 
 
 def solution(mesh):

time: 150 us -> 154 us (1.027)
  Pallas kernels: 138 us -> 153 us
  other arithmetic: 6.41 us -> 0 us
  local copies, waits for them, and re-layouts: 3.53 us -> 0 us
    pallas_call x0 -> x1, Pallas kernels: none -> 33.7 us  [shards(): pl.pallas_call(outer_kernel, out_shape=(jax.ShapeDtypeStruct((1, 1, 512,...]
    pallas_call x1, Pallas kernels: 138 us -> 119 us  [path_step(): pl.pallas_call(kernel, out_shape=(jax.ShapeDtypeStruct((1, 1, 512, 1024),...]
    convert_element_type x2 -> x0, other arithmetic: 5.17 us -> none  [the longest x1 2.61 us: shards(): (in_frag - OUTER_LR * (delta_in + MOMENTUM * new_mom_in)).astype(BF)]
where the time goes in v2:
time: 154 us; the launch traced here: 153 us
  Pallas kernels  153 us (99%)
    pallas_call x1, Pallas kernels, path_step(): pl.pallas_call(kernel, out_shape=(jax.ShapeDtypeStruct((1, 1, 512, 1024),...  119 us
    pallas_call x1, Pallas kernels, shards(): pl.pallas_call(outer_kernel, out_shape=(jax.ShapeDtypeStruct((1, 1, 512,...  33.7 us

profile of v2, /device:TPU:1, one launch (start us, length us, event | category | flops | bytes accessed | tf_op | source)
XLA Modules:
  0.0 153.5 jit_solution(5392304179783672546)
XLA Ops:
  0.6 119.2 %path_step.1 = (bf16[1,1,512,1024]{3,2,1,0:T(8,128)(2,1)}, bf16[4,2,128,256]{3,2,1,0:T(8,128)(2,1)}, bf16[2,4,128,256]{3,2,1,0:T(8,128)(2,1)}) custom-call(s32[16]{0:T(128)} %frag.3, bf16[1,1,512,1024]{3,2,1,0:T(8,128)(2,1)} %tok_hbm.1, bf16[1,1,512,1024]{3,2,1,0:T(8,128)(2,1)} %cot_hbm.1, bf16[1,256,4096]{2,1,0:T(8,128)(2,1)} %win_hbm.3, ...), custom_call_target="tpu_custom_call" | custom-call | flops 12884901888 | bytes 25165824 | tf_op jit(solution)/shard_map/path_step/pallas_call | solution.py:634
  119.8 33.7 %outer_update.1 = (bf16[1,1,512,1024]{3,2,1,0:T(8,128)(2,1)}, bf16[1,256,1024]{2,1,0:T(8,128)(2,1)}, f32[1,256,1024]{2,1,0:T(8,128)}, bf16[1,1024,256]{2,1,0:T(8,128)(2,1)}, f32[1,1024,256]{2,1,0:T(8,128)}) custom-call(s32[16]{0:T(128)} %frag.3, bf16[1,1,512,1024]{3,2,1,0:T(8,128)(2,1)} %get-tuple-element.8.mix_hbm, ...), custom_call_target="tpu_custom_call" | custom-call | flops 4194304 | bytes 9437184 | tf_op jit(solution)/shard_map/outer_update/pallas_call | solution.py:702

commit v3 on v2

--- a/solution.py
+++ b/solution.py
@@ -653,7 +653,7 @@
 def outer_kernel(
     frag, mix_hbm, sin_hbm, sout_hbm, win_hbm, wout_hbm, min_hbm, mout_hbm,
     mixed, new_in, new_mom_in, new_out, new_mom_out,
-    SIN, SOUT, WI, WO, MI, MO, NI, NMI, NO, NMO, sems,
+    SIN, SOUT, WI, WO, MI, MO, NI, NMI, NO, NMO, MX, sems,
 ):
     start_in = pl.multiple_of(frag[lax.axis_index("row")] * FU, FU)
     start_out = pl.multiple_of(frag[lax.axis_size("row") + lax.axis_index("col")] * FU, FU)
@@ -667,7 +667,8 @@
 
     first = [move(min_hbm.at[0], MI), move(win_hbm.at[0, :, pl.ds(start_in, FU)], WI), move(sin_hbm, SIN)]
     second = [move(mout_hbm.at[0], MO), move(wout_hbm.at[0, pl.ds(start_out, FU), :], WO), move(sout_hbm, SOUT)]
-    last = [move(mix_hbm, mixed)]
+    window = move(mix_hbm, MX)
+    last = []
 
     def update(delta, mom, frag_now):
         delta = INNER_LR * delta.astype(F32)
@@ -681,6 +682,8 @@
             at = (slice(h * 128, h * 128 + 128), slice(u * 256, u * 256 + 256))
             NMI[at], NI[at] = update(SIN[u, h], MI[at], WI[at])
     last += [move(NMI, new_mom_in.at[0]), move(NI, new_in.at[0])]
+    window.wait()
+    last.append(move(MX, mixed))
     for copy in second:
         copy.wait()
     for h in range(2):
@@ -697,7 +700,7 @@
     anywhere = pl.BlockSpec(memory_space=pl.ANY)
     sizes = [
         ((4, 2, 128, 256), BF), ((2, 4, 128, 256), BF), ((256, FU), BF), ((FU, 256), BF), ((256, FU), F32),
-        ((FU, 256), F32), ((256, FU), BF), ((256, FU), F32), ((FU, 256), BF), ((FU, 256), F32),
+        ((FU, 256), F32), ((256, FU), BF), ((256, FU), F32), ((FU, 256), BF), ((FU, 256), F32), ((1, 1, 512, 1024), BF),
     ]
     return pl.pallas_call(
         outer_kernel,

time: 154 us -> 125 us (0.81)
  Pallas kernels: 153 us -> 124 us
    pallas_call x1, Pallas kernels: 33.7 us -> 4.77 us  [shards(): pl.pallas_call(outer_kernel, out_shape=(jax.ShapeDtypeStruct((1, 1, 512,...]
where the time goes in v3:
time: 125 us
  Pallas kernels  124 us (99%)
    pallas_call x1, Pallas kernels, path_step(): pl.pallas_call(kernel, out_shape=(jax.ShapeDtypeStruct((1, 1, 512, 1024),...  119 us
    pallas_call x1, Pallas kernels, shards(): pl.pallas_call(outer_kernel, out_shape=(jax.ShapeDtypeStruct((1, 1, 512,...  4.77 us

profile of v3, /device:TPU:1, one launch (start us, length us, event | category | flops | bytes accessed | tf_op | source)
XLA Modules:
  0.0 124.6 jit_solution(17603172459721911966)
XLA Ops:
  0.6 119.2 %path_step.1 = (bf16[1,1,512,1024]{3,2,1,0:T(8,128)(2,1)}, bf16[4,2,128,256]{3,2,1,0:T(8,128)(2,1)}, bf16[2,4,128,256]{3,2,1,0:T(8,128)(2,1)}) custom-call(s32[16]{0:T(128)} %frag.3, bf16[1,1,512,1024]{3,2,1,0:T(8,128)(2,1)} %tok_hbm.1, bf16[1,1,512,1024]{3,2,1,0:T(8,128)(2,1)} %cot_hbm.1, bf16[1,256,4096]{2,1,0:T(8,128)(2,1)} %win_hbm.3, ...), custom_call_target="tpu_custom_call" | custom-call | flops 12884901888 | bytes 25165824 | tf_op jit(solution)/shard_map/path_step/pallas_call | solution.py:634
  119.8 4.8 %outer_update.1 = (bf16[1,1,512,1024]{3,2,1,0:T(8,128)(2,1)}, bf16[1,256,1024]{2,1,0:T(8,128)(2,1)}, f32[1,256,1024]{2,1,0:T(8,128)}, bf16[1,1024,256]{2,1,0:T(8,128)(2,1)}, f32[1,1024,256]{2,1,0:T(8,128)}) custom-call(s32[16]{0:T(128)} %frag.3, bf16[1,1,512,1024]{3,2,1,0:T(8,128)(2,1)} %get-tuple-element.8.mix_hbm, ...), custom_call_target="tpu_custom_call" | custom-call | flops 4194304 | bytes 9437184 | tf_op jit(solution)/shard_map/outer_update/pallas_call | solution.py:705

commit v4 on v3

--- a/solution.py
+++ b/solution.py
@@ -56,7 +56,7 @@
 
 class Copies:
     def __init__(self, send, recv):
-        self.send, self.recv, self.sent, self.ids = send, recv, [], {}
+        self.send, self.recv, self.sent, self.ids, self.flushed = send, recv, [], {}, 0
 
     def at(self, name):
         return self.recv.at[self.ids.setdefault(name, len(self.ids))]
@@ -76,9 +76,10 @@
             device_id=self.sent[0].device_id, device_id_type=MESH,
         ).wait_recv()
 
-    def flush(self):
-        for copy in self.sent:
+    def flush(self, end):
+        for copy in self.sent[self.flushed : end]:
             copy.wait_send()
+        self.flushed = end
 
 
 def gelu(v):
@@ -130,7 +131,6 @@
     partners = p.partners()
     for dev in partners:
         pl.semaphore_signal(barrier, inc=1, device_id=dev, device_id_type=MESH)
-    pl.semaphore_wait(barrier, len(partners))
 
     near, twin, sib = p.near(), p.twin(), p.sib()
     shard = {"n": (s + p.turn + 4) % 4, "t": (s - p.turn + 4) % 4, "f": (s + 2) % 4}
@@ -142,10 +142,10 @@
             return WOUT.at[f, o // 2, rows((o % 2) * 512, 512), :]
         return WOUT.at[f, o // 2, rows((o % 2) * 512 + g * 256, 256), :]
 
-    def s_start():
-        mine = wout_hbm.at[0, rows(r * 512, 512), :]
-        C.put("s1m", mine, wo(s, r), p.at_s(1))
-        C.put("s1p", mine, wo(s, r), p.at_s(-1))
+    mine = wout_hbm.at[0, rows(r * 512, 512), :]
+
+    def s_start(side):
+        C.put(f"s1{side}", mine, wo(s, r), p.at_s(1 if side == "m" else -1))
 
     def s_hop(side):
         if side == "m":
@@ -167,16 +167,12 @@
         C.put(f"xp{f}", ref, ref, p.at_x(-1))
         C.put(f"c0{f}", ref, ref, sib)
 
-    def x_hop(f):
-        a, b = wo(so[f], ox["m"]), wo(so[f], ox["p"])
-        C.got(f"xm{f}", a)
-        ref = wo(so[f], ox["m"], 0)
-        C.put(f"vm{f}", ref, ref, p.at_x(1))
-        C.got(f"xp{f}", b)
-        ref = wo(so[f], ox["p"], 1)
-        C.put(f"vp{f}", ref, ref, p.at_x(-1))
-        C.put(f"cm{f}", a, a, sib)
-        C.put(f"cp{f}", b, b, sib)
+    def x_hop(side, f):
+        a = wo(so[f], ox[side])
+        C.got(f"x{side}{f}", a)
+        ref = wo(so[f], ox[side], 0 if side == "m" else 1)
+        C.put(f"v{side}{f}", ref, ref, p.at_x(1 if side == "m" else -1))
+        C.put(f"c{side}{f}", a, a, sib)
 
     def x_last(f):
         C.got(f"vm{f}", wo(so[f], ox["f"], 0))
@@ -204,31 +200,21 @@
         ref = zc(t, s, second)
         C.put(f"z{t}nA", ref, ref, near)
 
-    def z_hop1(t):
-        ref = zc(t, shard["n"], first)
-        C.got(f"z{t}nA", ref)
-        C.put(f"z{t}tB", ref, ref, twin)
-        ref = zc(t, shard["n"], second)
-        C.got(f"z{t}nB", ref)
-        C.put(f"z{t}tA", ref, ref, twin)
-        y_send(t, "n")
+    def z_hop1(t, role):
+        ref = zc(t, shard["n"], first if role == "A" else second)
+        C.got(f"z{t}n{role}", ref)
+        C.put(f"z{t}t" + ("B" if role == "A" else "A"), ref, ref, twin)
 
     def z_hop2(t):
         ref = zc(t, shard["t"], second)
         C.got(f"z{t}tB", ref)
         C.put(f"z{t}fA", ref, ref, near)
-        C.got(f"z{t}tA", zc(t, shard["t"], first))
-        y_send(t, "t")
 
     def z_hop3(t):
         ref = zc(t, shard["f"], first)
         C.got(f"z{t}fA", ref)
         C.put(f"z{t}fB", ref, ref, twin)
 
-    def z_hop4(t):
-        C.got(f"z{t}fB", zc(t, shard["f"], second))
-        y_send(t, "f")
-
     def blk(t, u, f, h=None):
         if h is None:
             return WIN.at[t, u, rows(shard[f] * 256, 256), :]
@@ -241,20 +227,21 @@
         return (y + 1) % 2 + 2 if DOUBLE[t] else yp
 
     def y_send(t, f):
+        if f == "t":
+            C.got(f"z{t}tA", zc(t, shard["t"], first))
+        if f == "f":
+            C.got(f"z{t}fB", zc(t, shard["f"], second))
         a = blk(t, y % 2 if DOUBLE[t] else y, f)
         b = blk(t, y % 2 + 2 if DOUBLE[t] else y, f)
         C.put(f"y{t}{f}m", a, a, p.at_y(1))
         C.put(f"y{t}{f}p", b, b, p.at_y(-1))
 
-    def y_hop(t, f):
-        C.got(f"y{t}{f}m", blk(t, from_m(t), f))
+    def y_hop(side, t, f):
+        at, h = (ym, 0) if side == "m" else (yp, 1)
+        C.got(f"y{t}{f}{side}", blk(t, from_m(t) if side == "m" else from_p(t), f))
         if not DOUBLE[t]:
-            ref = blk(t, ym, f, 0)
-            C.put(f"w{t}{f}m", ref, ref, p.at_y(1))
-        C.got(f"y{t}{f}p", blk(t, from_p(t), f))
-        if not DOUBLE[t]:
-            ref = blk(t, yp, f, 1)
-            C.put(f"w{t}{f}p", ref, ref, p.at_y(-1))
+            ref = blk(t, at, f, h)
+            C.put(f"w{t}{f}{side}", ref, ref, p.at_y(1 if side == "m" else -1))
 
     def y_last(t):
         if not DOUBLE[t]:
@@ -344,7 +331,7 @@
             GIB[1, HI, :] = (GIB[1, HI, :].astype(F32) + RA[1].astype(F32)).astype(BF)
             C.put("ai5", GIB.at[1, HI], RA.at[5], p.at_y(-1))
 
-    zs = [(d, e) for d in range(4) for e in range(2) if (d, e) != (0, 0)]
+    zs = [(2, 0), (2, 1), (1, 1), (3, 1), (1, 0), (3, 0), (0, 1)]
 
     def in_sum():
         C.got("ai2", RA.at[2])
@@ -486,68 +473,96 @@
 
         mix_out.append(load(MIX.at[:, pl.ds(b * 256, 256)], mix_hbm.at[0, 0, :, pl.ds(b * 256, 256)]))
 
-    s_start()
     for copy in own_in:
         copy.wait()
     place_own(0)
+    place_own(1)
+    pl.semaphore_wait(barrier, len(partners))
+    s_start("m")
+    s_start("p")
     z_start(0)
-    place_own(1)
-    z_hop1(0)
+    z_hop1(0, "A")
+    z_hop1(0, "B")
+    y_send(0, "n")
     z_start(1)
     z_hop2(0)
+    y_send(0, "t")
     place_own(2)
     z_start(2)
-    z_hop1(1)
+    z_hop1(1, "A")
+    z_hop1(1, "B")
+    y_send(1, "n")
     normalize()
     z_hop3(0)
     s_hop("m")
     x_send("m")
     z_hop2(1)
-    y_hop(0, "t")
-    y_hop(0, "n")
+    y_send(1, "t")
+    y_hop("m", 0, "t")
+    y_hop("p", 0, "t")
+    y_hop("m", 0, "n")
+    y_hop("p", 0, "n")
     s_hop("p")
-    z_hop4(0)
+    y_send(0, "f")
     x_send("p")
     place_own(3)
     transpose_normed()
-    y_hop(1, "t")
-    y_hop(1, "n")
+    y_hop("m", 1, "t")
+    y_hop("p", 1, "t")
+    y_hop("m", 1, "n")
+    y_hop("p", 1, "n")
     z_start(3)
-    z_hop1(2)
+    z_hop1(2, "A")
+    z_hop1(2, "B")
+    y_send(2, "n")
     s_last()
     x_send("f")
     z_hop3(1)
-    y_hop(0, "f")
-    z_hop1(3)
-    x_hop("m")
+    y_hop("m", 0, "f")
+    y_hop("p", 0, "f")
+    z_hop1(3, "A")
+    z_hop1(3, "B")
+    y_send(3, "n")
+    x_hop("m", "m")
+    x_hop("p", "m")
     z_hop2(2)
-    z_hop4(1)
-    x_hop("f")
+    y_send(2, "t")
+    y_send(1, "f")
+    x_hop("m", "f")
+    x_hop("p", "f")
     z_hop3(2)
-    x_hop("p")
+    x_hop("m", "p")
+    x_hop("p", "p")
     z_hop2(3)
-    y_hop(2, "n")
+    y_send(3, "t")
+    y_hop("m", 2, "n")
+    y_hop("p", 2, "n")
     up(1, block_at(1, 0))
     up(0, block_at(0, 1))
     x_last("f")
     x_last("m")
-    z_hop4(2)
+    y_send(2, "f")
     up(0, block_at(0, 0))
     x_last("p")
-    y_hop(2, "t")
+    y_hop("m", 2, "t")
+    y_hop("p", 2, "t")
     z_hop3(3)
     up(2, block_at(2, 0))
     y_last(0)
     up(0, block_at(0, 3))
     up(0, block_at(0, 2))
     core_last()
-    y_hop(1, "f")
+    y_hop("m", 1, "f")
+    y_hop("p", 1, "f")
     take_fragment()
-    y_hop(2, "f")
-    y_hop(3, "t")
+    y_hop("m", 2, "f")
+    y_hop("p", 2, "f")
+    y_hop("m", 3, "t")
+    y_hop("p", 3, "t")
     y_last(2)
-    z_hop4(3)
-    y_hop(3, "n")
+    y_send(3, "f")
+    y_hop("m", 3, "n")
+    y_hop("p", 3, "n")
     up(3, block_at(3, 1))
     cot_in.wait()
     in_part(0)
@@ -560,12 +575,14 @@
     in_part(2)
     up(1, block_at(1, 1))
     up(1, block_at(1, 3))
-    y_hop(3, "f")
+    y_hop("m", 3, "f")
+    y_hop("p", 3, "f")
     y_last(3)
     up(3, block_at(3, 2))
     up(2, block_at(2, 2))
     up(3, block_at(3, 3))
     in_relay(1)
+    gathered = len(C.sent)
     out_start(0)
     in_relay(0)
     out_start(1)
@@ -574,6 +591,7 @@
     out_reduce()
     in_sum()
     in_place()
+    C.flush(gathered)
     down(1)
     out_relay()
     out_sum()
@@ -587,9 +605,10 @@
     out_spread()
     out_last()
     in_last()
-
-    stores = [load(FIN, fin_hbm), load(FOUT, fout_hbm)]
-    C.flush()
+    stores = [load(FIN, fin_hbm)]
+
+    stores.append(load(FOUT, fout_hbm))
+    C.flush(len(C.sent))
     for copy in stores:
         copy.wait()
     for copy in mix_out:

time: 125 us -> 125 us (level)
  no operation moved by 1% of the time
where the time goes in v4:
time: 125 us
  Pallas kernels  124 us (99%)
    pallas_call x1, Pallas kernels, path_step(): pl.pallas_call(kernel, out_shape=(jax.ShapeDtypeStruct((1, 1, 512, 1024),...  119 us
    pallas_call x1, Pallas kernels, shards(): pl.pallas_call(outer_kernel, out_shape=(jax.ShapeDtypeStruct((1, 1, 512,...  4.75 us

profile of v4, /device:TPU:1, one launch (start us, length us, event | category | flops | bytes accessed | tf_op | source)
XLA Modules:
  0.0 124.6 jit_solution(2287361061881378966)
XLA Ops:
  0.6 119.2 %path_step.1 = (bf16[1,1,512,1024]{3,2,1,0:T(8,128)(2,1)}, bf16[4,2,128,256]{3,2,1,0:T(8,128)(2,1)}, bf16[2,4,128,256]{3,2,1,0:T(8,128)(2,1)}) custom-call(s32[16]{0:T(128)} %frag.3, bf16[1,1,512,1024]{3,2,1,0:T(8,128)(2,1)} %tok_hbm.1, bf16[1,1,512,1024]{3,2,1,0:T(8,128)(2,1)} %cot_hbm.1, bf16[1,256,4096]{2,1,0:T(8,128)(2,1)} %win_hbm.3, ...), custom_call_target="tpu_custom_call" | custom-call | flops 12884901888 | bytes 25165824 | tf_op jit(solution)/shard_map/path_step/pallas_call | solution.py:653
  119.9 4.7 %outer_update.1 = (bf16[1,1,512,1024]{3,2,1,0:T(8,128)(2,1)}, bf16[1,256,1024]{2,1,0:T(8,128)(2,1)}, f32[1,256,1024]{2,1,0:T(8,128)}, bf16[1,1024,256]{2,1,0:T(8,128)(2,1)}, f32[1,1024,256]{2,1,0:T(8,128)}) custom-call(s32[16]{0:T(128)} %frag.3, bf16[1,1,512,1024]{3,2,1,0:T(8,128)(2,1)} %get-tuple-element.8.mix_hbm, ...), custom_call_target="tpu_custom_call" | custom-call | flops 4194304 | bytes 9437184 | tf_op jit(solution)/shard_map/outer_update/pallas_call | solution.py:724
